TPU v7x, 512 devices: a whole 4x8x8 slice. The times are simulated.
512 devices in a mesh: table: 8 (over y), batch: 64 (over z, x, core).
Axes of the slice: x: 4, y: 8, z: 8, core: 2. Of those that a mesh axis runs over, the one named last changes fastest.
Arguments:
- table: bfloat16 [8192, 512], P('table'), may hold values from -6 to 6
- owner: int32 [131072, 1], P(('table', 'batch')), may hold values from 0 to 7; in each aligned block of 256 rows (0 to 255, 256 to 511, ...) at most 48 rows name the same one
- local_row: int32 [131072], P(('table', 'batch')), may hold values from 0 to 1023
- lengths: int32 [512, 2], P(('table', 'batch')), may hold values from 1 to 192, 256 in all within a row
- w_in: bfloat16 [512, 2048], replicated, may hold values from -0.25 to 0.25
- w_out: bfloat16 [512, 512], replicated, may hold values from -0.25 to 0.25
- cotangent: bfloat16 [131072, 512], P(('table', 'batch')), may hold values from -0.59765625 to 0.59765625
Outputs:
- layer_out: bfloat16 [131072, 512], P(('table', 'batch'))
- table_grad: float32 [8192, 512], P(('table', 'batch'))
- w_out_grad: bfloat16 [512, 512], P('batch')
Inputs may be any that keep to these rules, and one draw needn't show every extreme that they name: `owner`: among the rows of one device no shard is named by more than 48 rows, and in every draw some device names some shard exactly 48 times. `lengths`: each row sums to 256; the largest entry of the whole array is 192.
All inputs are finite; a program needn't handle non-finite values.
Results may differ from a plain program's by a relative error of at most 0.017.
Values may be sent and summed in bfloat16 or wider, within the bound.
A program may use at most 64 MiB of HBM per device.

v0:
```python
import jax
import jax.numpy as jnp
from jax import lax
from jax.sharding import PartitionSpec as P

HEADS = 8
MOST_LEN = 192


EPSILON = 1e-05


def layer_norm(values):
    center = jnp.mean(values, axis=-1, keepdims=True)
    spread = jnp.mean((values - center) * (values - center), axis=-1, keepdims=True)
    return (values - center) * lax.rsqrt(spread + EPSILON)


def hstu_block(embedded, history, w_in, w_out):
    count, width = embedded.shape
    head_size = width // HEADS
    inputs = embedded.astype(jnp.float32)
    normed = layer_norm(inputs).astype(jnp.bfloat16)
    hidden = jnp.dot(normed, w_in, preferred_element_type=jnp.float32)
    branches = jax.nn.silu(hidden).astype(jnp.bfloat16)
    gate_part = branches[:, :width]
    value_part = branches[:, width : 2 * width].reshape(count, HEADS, head_size)
    query_part = branches[:, 2 * width : 3 * width].reshape(count, HEADS, head_size)
    key_part = branches[:, 3 * width :].reshape(count, HEADS, head_size)
    scores = jnp.einsum(
        "ihe,jhe->hij", query_part, key_part, preferred_element_type=jnp.float32
    ) * head_size ** (-0.5)
    places = jnp.arange(count)
    allowed = (history[:, None] == history[None, :]) & (places[None, :] <= places[:, None])
    weights = jnp.where(allowed[None], jax.nn.silu(scores) / MOST_LEN, 0.0).astype(jnp.bfloat16)
    attended = jnp.einsum(
        "hij,jhe->ihe", weights, value_part, preferred_element_type=jnp.float32
    ).reshape(count, width)
    gated = (layer_norm(attended) * gate_part.astype(jnp.float32)).astype(jnp.bfloat16)
    result = (jnp.dot(gated, w_out, preferred_element_type=jnp.float32) + inputs).astype(
        jnp.bfloat16
    )
    return (result, gated)


def on_device(table, owner, local_row, lengths, w_in, w_out, cotangent):
    count, width = cotangent.shape
    rows_dev = table.shape[0]
    shard_count = lax.axis_size("table")
    capacity = min(count, 3 * count // (2 * shard_count))
    column = owner[:, 0]
    onehot = (column[:, None] == jnp.arange(shard_count)[None, :]).astype(jnp.int32)
    rank = jnp.sum(jnp.cumsum(onehot, axis=0) * onehot, axis=1) - 1
    requests = jnp.zeros((shard_count, capacity), jnp.int32).at[column, rank].set(local_row)
    wanted = lax.all_to_all(requests, "table", split_axis=0, concat_axis=0, tiled=True)
    replies = jnp.take(table, wanted, axis=0)
    fetched = lax.all_to_all(replies, "table", split_axis=0, concat_axis=0, tiled=True)
    embedded = fetched[column, rank]
    bounds = jnp.cumsum(lengths[0])
    history = jnp.sum((jnp.arange(count)[:, None] >= bounds[None, :]).astype(jnp.int32), axis=1)
    result, pullback, gated = jax.vjp(
        lambda values: hstu_block(values, history, w_in, w_out), embedded, has_aux=True
    )
    token_grads = pullback(cotangent)[0]
    grad_slots = (
        jnp.zeros((shard_count, capacity, width), jnp.bfloat16).at[column, rank].set(token_grads)
    )
    returned = lax.all_to_all(grad_slots, "table", split_axis=0, concat_axis=0, tiled=True)
    dense = (
        jnp.zeros((rows_dev, width), jnp.float32)
        .at[wanted.reshape(-1)]
        .add(returned.reshape(-1, width).astype(jnp.float32))
    )
    table_grad = lax.psum_scatter(dense, "batch", scatter_dimension=0, tiled=True)
    slice_rows = width // lax.axis_size("batch")
    local_term = jnp.einsum("td,te->de", gated, cotangent, preferred_element_type=jnp.float32)
    summed = lax.psum(local_term, ("table", "batch"))
    weight_grad = lax.dynamic_slice_in_dim(
        summed, lax.axis_index("batch") * slice_rows, slice_rows, 0
    )
    return (result, table_grad, weight_grad.astype(jnp.bfloat16))


def solution(mesh):
    return jax.shard_map(
        on_device,
        mesh=mesh,
        in_specs=(
            P("table", None),
            P(("table", "batch"), None),
            P(("table", "batch")),
            P(("table", "batch"), None),
            P(),
            P(),
            P(("table", "batch"), None),
        ),
        out_specs=(P(("table", "batch"), None), P(("table", "batch"), None), P("batch", None)),
        check_vma=False,
    )
```

profile of v0, /device:TPU:1, one launch (start us, length us, event | category | flops | bytes accessed | tf_op | source)
XLA Modules:
  0.0 295.5 jit_solution(13170418251826649895)
XLA Ops:
  7.2 0.8 fusion.45
  10.3 21.4 %scatter_fusion = s32[8,48]{1,0:T(8,128)S(1)} fusion(s32[8,48]{1,0:T(8,128)S(1)} %broadcast_in_dim.68, s32[256]{0:T(256)S(1)} %bitcast.68, s32[256]{0:T(256)} %param.9), kind=kCustom, calls=%fused_computation.2 | custom fusion | bytes 5120 | tf_op jit(solution)/shard_map/scatter | solution.py:54
  31.8 14.0 %all_to_all.25 = s32[8,1,48]{2,1,0:T(1,128)S(1)} all-to-all(s32[8,1,48]{2,1,0:T(1,128)S(1)} %bitcast.67), channel_id=1, replica_groups=mesh['table'=8,'batch'=64] {'table'}, dimensions={0} | all-to-all | bytes 3072 | tf_op jit(solution)/shard_map/all_to_all | solution.py:55
  45.9 2.6 gather_fusion
  48.5 1.9 broadcast_select_fusion
  50.3 3.5 %all-to-all-start.1 = ((bf16[8,48,512]{2,1,0:T(8,128)(2,1)}), bf16[8,48,512]{2,1,0:T(8,128)(2,1)S(1)}, u32[]{:S(2)}, u32[]{:S(2)}) async-start(bf16[8,48,512]{2,1,0:T(8,128)(2,1)} %broadcast_select_fusion), calls=%async_computation.1 | async-start | bytes 786432 | tf_op jit(solution)/shard_map/all_to_all | solution.py:57
  54.2 10.3 %all-to-all-done.1 = bf16[8,48,512]{2,1,0:T(8,128)(2,1)S(1)} async-done(((bf16[8,48,512]{2,1,0:T(8,128)(2,1)}), bf16[8,48,512]{2,1,0:T(8,128)(2,1)S(1)}, u32[]{:S(2)}, u32[]{:S(2)}) %all-to-all-start.1) | async-done | bytes 393248 | tf_op jit(solution)/shard_map/all_to_all | solution.py:57
  64.5 2.1 gather_fusion.1
  66.9 2.1 multiply_convert_fusion
  69.1 1.0 copy-done.5
  70.5 2.2 select_convert_fusion
  74.1 2.4 multiply_reduce_fusion.4
  76.6 1.2 fusion.36
  77.9 3.0 %fusion.7 = bf16[8,256,256]{2,1,0:T(8,128)(2,1)S(1)} fusion(f32[8,256,256]{2,1,0:T(8,128)} %get-tuple-element.19, bf16[8,64,256]{2,1,0:T(8,128)(2,1)S(1)} %bitcast.80, bf16[256,8,64]{0,2,1:T(8,128)(2,1)} %bitcast.75, pred[256,256]{1,0:T(8,128)(4,1)S(1)} %fusion.43), kind=kOutput, calls=%fused_computation.14 | convolution fusion | flops 74973184 | bytes 3735552 | tf_op jit(solution)/shard_map/transpose(jvp(hij,jhe->ihe))/dot_general | solution.py:36
  83.0 2.8 multiply_reduce_fusion.3
  87.1 33.0 %scatter_fusion.1 = bf16[8,48,512]{2,1,0:T(8,128)(2,1)} fusion(bf16[8,48,512]{2,1,0:T(8,128)(2,1)} %broadcast_in_dim.75, s32[256]{0:T(256)S(1)} %bitcast.69, bf16[256,512]{1,0:T(8,128)(2,1)S(1)} %fusion.38), kind=kCustom, calls=%fused_computation.3 | custom fusion | bytes 788480 | tf_op jit(solution)/shard_map/scatter | solution.py:66
  120.1 3.7 %all-to-all-start.2 = ((bf16[8,48,512]{2,1,0:T(8,128)(2,1)}), bf16[8,48,512]{2,1,0:T(8,128)(2,1)S(1)}, u32[]{:S(2)}, u32[]{:S(2)}) async-start(bf16[8,48,512]{2,1,0:T(8,128)(2,1)} %scatter_fusion.1), calls=%async_computation.2 | async-start | bytes 786432 | tf_op jit(solution)/shard_map/all_to_all | solution.py:68
  125.3 9.2 %all-to-all-done.2 = bf16[8,48,512]{2,1,0:T(8,128)(2,1)S(1)} async-done(((bf16[8,48,512]{2,1,0:T(8,128)(2,1)}), bf16[8,48,512]{2,1,0:T(8,128)(2,1)S(1)}, u32[]{:S(2)}, u32[]{:S(2)}) %all-to-all-start.2) | async-done | bytes 393248 | tf_op jit(solution)/shard_map/all_to_all | solution.py:68
  134.5 4.5 %scatter_custom_fusion.2 = f32[1024,512]{1,0:T(8,128)} fusion(s32[384]{0:T(512)S(1)} %fusion.47, f32[]{:T(128)} %constant.66.clone.1, bf16[384,512]{1,0:T(8,128)(2,1)S(1)} %bitcast.72), kind=kCustom, calls=%fused_computation.36 | custom fusion | flops 393216 | bytes 2490372 | tf_op jit(solution)/shard_map/scatter-add | solution.py:72
  139.0 1.4 fusion.58
  140.4 113.3 %all-reduce.5 = bf16[512,512]{1,0:T(8,128)(2,1)} all-reduce(f32[512,512]{1,0:T(8,128)S(1)} %fusion.58), channel_id=1, replica_groups=mesh['table'=8,'batch'=64] {'table','batch'}, use_global_device_ids=true, to_apply=%region_19.20 | all-reduce | flops 262144 | bytes 1572864 | tf_op jit(solution)/shard_map/psum | solution.py:77
  253.7 1.3 dynamic-slice_convert_fusion
  255.0 2.1 fusion.8
  257.1 31.5 %reduce-scatter.2.cloned.1.call-done = f32[16,512]{1,0:T(8,128)} async-done(((f32[1024,512]{1,0:T(8,128)}), f32[16,512]{1,0:T(8,128)}) %reduce-scatter.2.cloned.1.call-update) | async-done | bytes 32784 | tf_op jit(solution)/shard_map/reduce_scatter | solution.py:74
  (72 shorter events, 9.9 us)
Async XLA Ops:
  7.2 59.7 %copy-start = (bf16[512,2048]{1,0:T(8,128)(2,1)S(1)}, bf16[512,2048]{1,0:T(8,128)(2,1)}, u32[]{:S(2)}) copy-start(bf16[512,2048]{1,0:T(8,128)(2,1)} %param.11) | copy-start | bytes 6291460
  7.2 38.7 %copy-start.1 = (bf16[1024,512]{1,0:T(8,128)(2,1)S(1)}, bf16[1024,512]{1,0:T(8,128)(2,1)}, u32[]{:S(2)}) copy-start(bf16[1024,512]{1,0:T(8,128)(2,1)} %param.7) | copy-start | bytes 3145732
  45.9 7.9 %copy-start.11 = (s32[1,2]{1,0:T(1,128)S(1)}, s32[1,2]{1,0:T(1,128)}, u32[]{:S(2)}) copy-start(s32[1,2]{1,0:T(1,128)} %param.10) | copy-start | bytes 28
  50.3 14.1 %all-to-all-start.1 = ((bf16[8,48,512]{2,1,0:T(8,128)(2,1)}), bf16[8,48,512]{2,1,0:T(8,128)(2,1)S(1)}, u32[]{:S(2)}, u32[]{:S(2)}) async-start(bf16[8,48,512]{2,1,0:T(8,128)(2,1)} %broadcast_select_fusion), calls=%async_computation.1 | async-start | bytes 786432 | tf_op jit(solution)/shard_map/all_to_all | solution.py:57
  69.1 1.0 copy-start.5
  70.2 2.5 copy-start.7
  70.4 2.3 copy-start.9
  70.5 2.2 copy-start.6
  72.7 1.0 copy-start.2
  77.9 3.1 %copy-start.8 = (bf16[256,512]{0,1:T(8,128)(2,1)S(1)}, bf16[256,512]{0,1:T(8,128)(2,1)}, u32[]{:S(2)}) copy-start(bf16[256,512]{0,1:T(8,128)(2,1)} %copy-done.7) | copy-start | bytes 786436
  77.9 3.4 %copy-start.10 = (bf16[256,512]{0,1:T(8,128)(2,1)S(1)}, bf16[256,512]{0,1:T(8,128)(2,1)}, u32[]{:S(2)}) copy-start(bf16[256,512]{0,1:T(8,128)(2,1)} %copy-done.9) | copy-start | bytes 786436
  81.0 1.2 copy-start.3
  82.9 3.1 %copy-start.4 = (bf16[256,512]{1,0:T(8,128)(2,1)S(1)}, bf16[256,512]{1,0:T(8,128)(2,1)}, u32[]{:S(2)}) copy-start(bf16[256,512]{1,0:T(8,128)(2,1)} %param.13) | copy-start | bytes 786436
  120.1 14.5 %all-to-all-start.2 = ((bf16[8,48,512]{2,1,0:T(8,128)(2,1)}), bf16[8,48,512]{2,1,0:T(8,128)(2,1)S(1)}, u32[]{:S(2)}, u32[]{:S(2)}) async-start(bf16[8,48,512]{2,1,0:T(8,128)(2,1)} %scatter_fusion.1), calls=%async_computation.2 | async-start | bytes 786432 | tf_op jit(solution)/shard_map/all_to_all | solution.py:68
  123.8 164.8 %reduce-scatter.2.cloned.1.call-start = ((), (), s32[]{:S(2)}) async-start(), calls=%async_computation.4 | async-start | bytes 2129920 | tf_op jit(solution)/shard_map/reduce_scatter | solution.py:74
Sparse Core Ops, SparseCore 0:
  139.2 149.4 reduce-scatter.1
where the time goes:
time: 301 us; the launch traced here: 295 us
  blocking collectives  127 us (42%)
  local copies, waits for them, and re-layouts  65.3 us (22%)
  waiting for transfers between devices  51 us (17%)
  matrix products  17.5 us (6%)
  between operations  14.4 us (5%)
  other arithmetic  12.5 us (4%)
  starting transfers between devices  7.38 us (2%)
    psum x1, blocking collectives, on_device(): summed = lax.psum(local_term, ('table', 'batch'))  113 us
    scatter x1, local copies, waits for them, and re-layouts, on_device(): jnp.zeros((shard_count, capacity, width), jnp.bfloat16).at[column, rank]  33 us
    reduce_scatter x1, waiting for transfers between devices, on_device(): lax.psum_scatter(dense, 'batch', scatter_dimension=0, tiled=True)  31.5 us
    scatter x1, local copies, waits for them, and re-layouts, on_device(): jnp.zeros((shard_count, capacity), jnp.int32).at[column, rank]  21.4 us
    all_to_all x1, blocking collectives, on_device(): lax.all_to_all(requests, 'table', split_axis=0, concat_axis=0, tiled=True)  14 us
    all_to_all x1, waiting for transfers between devices, on_device(): lax.all_to_all(replies, 'table', split_axis=0, concat_axis=0, tiled=True)  10.3 us
    all_to_all x1, waiting for transfers between devices, on_device(): lax.all_to_all(grad_slots, 'table', split_axis=0, concat_axis=0, tiled=True)  9.24 us
  transfers between devices with their start and end apart: 3, of which 3 were waited for; matrix products, arithmetic and copies ran while one was open for 2% of the time, Pallas kernels for 0%

commit v1 on v0

v1 whole, which is shorter than its diff:
```python
import functools

import jax
import jax.numpy as jnp
from jax import lax
from jax.experimental import pallas as pl
from jax.experimental.pallas import tpu as pltpu
from jax.sharding import PartitionSpec as P

HEADS = 8
MOST_LEN = 192
EPSILON = 1e-05
CORES = 2
F32 = jnp.float32
BF16 = jnp.bfloat16


def dot(a, b):
    return lax.dot_general(a, b, (((1,), (0,)), ((), ())), preferred_element_type=F32)


def dot_nt(a, b):
    return lax.dot_general(a, b, (((1,), (1,)), ((), ())), preferred_element_type=F32)


def dot_tn(a, b):
    return lax.dot_general(a, b, (((0,), (0,)), ((), ())), preferred_element_type=F32)


def iota(shape, dim):
    return lax.broadcasted_iota(jnp.int32, shape, dim)


def sigmoid(z):
    return 0.5 * jnp.tanh(0.5 * z) + 0.5


def far_first(n):
    return sorted(range(n), key=lambda d: -min(d, n - d))


def kernel(
    ny, nz, nx, cap,
    owner_hbm, row_hbm, len_hbm, table_hbm, w_in_hbm, w_out_hbm, cot_hbm,
    out_hbm, tgrad_ref, wgrad_ref,
    owner_ref, row_ref, len_ref, table, w_in, w_out, cot, out,
    idx_own, idx_all, reply, fetched, place, hot,
    branch, slope, weight, sslope, sides,
    packed, ret, half_out, half_in, rs_out, rs_in,
    wsw_out, wsw_in, wrs_out, wrs_in, way_out, way_in, wfin_out, wfin_in,
    load_sem, store_sem, send_sem, recv_sem,
):
    tok, width = cot.shape
    nc = CORES
    pair_width = 128
    pairs = width // pair_width
    chunk = width // nx
    half_width = width // nc
    slots = ny * cap
    listed_width = idx_own.shape[-1]
    y = lax.axis_index("table")
    b = lax.axis_index("batch")
    core = b % nc
    x = (b // nc) % nx
    z = b // (nc * nx)
    zx = z * nx + x
    sibling = {"table": y, "batch": zx * nc + (1 - core)}

    def device(yy, zz, xx):
        return {"table": yy, "batch": (zz * nx + xx) * nc + core}

    columns = [(dy, dx) for dy in far_first(ny) for dx in far_first(nx) if (dy, dx) != (0, 0)]
    planes = [(dz, dx) for dz in far_first(nz) for dx in far_first(nx) if (dz, dx) != (0, 0)]

    def in_column(dy, dx):
        return (y + dy) & (ny - 1), (x + dx) & (nx - 1)

    def in_plane(dz, dx):
        return (z + dz) & (nz - 1), (x + dx) & (nx - 1)

    barrier = pltpu.get_barrier_semaphore()
    greeted = 0
    for dy, dx in columns:
        yy, xx = in_column(dy, dx)
        pl.semaphore_signal(barrier, inc=1, device_id=device(yy, z, xx))
        greeted += 1
    for dz, dx in planes:
        if dz == 0:
            continue
        zz, xx = in_plane(dz, dx)
        pl.semaphore_signal(barrier, inc=1, device_id=device(y, zz, xx))
        greeted += 1
    pl.semaphore_signal(barrier, inc=1, device_id=sibling)
    greeted += 1

    loads = [
        pltpu.make_async_copy(src, dst, load_sem.at[i])
        for i, (src, dst) in enumerate(
            [
                (owner_hbm, owner_ref),
                (row_hbm, row_ref),
                (table_hbm, table),
                (len_hbm, len_ref),
                (cot_hbm, cot),
                (w_out_hbm, w_out),
                (w_in_hbm, w_in),
            ]
        )
    ]
    for load in loads:
        load.start()

    loads[0].wait()
    loads[1].wait()
    owner = owner_ref[...]
    rows = row_ref[...]
    mine = (iota((ny, tok), 0) == owner).astype(F32)
    earlier = (iota((tok, tok), 0) < iota((tok, tok), 1)).astype(F32).astype(BF16)
    before = dot(mine.astype(BF16), earlier)
    rank = jnp.sum(mine * before, axis=0, keepdims=True).astype(jnp.int32)
    rank_hot = (iota((listed_width, tok), 0) == rank).astype(F32).astype(BF16)
    high = (rows // 32).astype(F32)
    low = (rows % 32).astype(F32)
    parts = jnp.concatenate([mine * high, mine * low], axis=0).astype(BF16)
    listed = dot_nt(parts, rank_hot)
    listed = (listed[:ny] * 32.0 + listed[ny:]).astype(jnp.int32)
    for o in range(ny):
        idx_own[o] = listed[o : o + 1]
    idx_all[x * ny + y] = idx_own[y]
    slot = owner * cap + rank
    place[...] = (iota((slots, tok), 0) == slot).astype(F32).astype(BF16)
    slot_col = jnp.broadcast_to(slot.astype(F32), (8, tok)).T[:, :1].astype(jnp.int32)
    unplace = (iota((tok, slots), 1) == slot_col).astype(F32).astype(BF16)

    pl.semaphore_wait(barrier, greeted)

    def send(src, dst, stage, target):
        copy = pltpu.make_async_remote_copy(
            src_ref=src,
            dst_ref=dst,
            send_sem=send_sem.at[stage],
            recv_sem=recv_sem.at[stage],
            device_id=target,
        )
        copy.start()

    def wait_recv(slab, stage):
        pltpu.make_async_copy(slab, slab, recv_sem.at[stage]).wait()

    def wait_send(slab, stage):
        pltpu.make_async_copy(slab, slab, send_sem.at[stage]).wait()

    near = [dy for dy in far_first(ny) if dy]
    for dy in near:
        yy, _ = in_column(dy, 0)
        send(idx_own.at[yy], idx_all.at[x * ny + y], 0, device(yy, z, x))
    loads[2].wait()
    wait_recv(idx_all.at[pl.ds(0, ny - 1)], 0)

    order = far_first(ny)
    asked = [idx_all[x * ny + ((y + dy) & (ny - 1))] for dy in order]
    if ny < 8:
        asked = asked + [asked[0]] * (8 - ny)
    asked = jnp.concatenate(asked, axis=0).astype(F32).T.astype(jnp.int32)
    shard_rows = table.shape[0]
    group = 2
    for g in range(0, ny, group):
        picks = jnp.concatenate(
            [iota((cap, shard_rows), 1) == asked[:cap, k : k + 1] for k in range(g, g + group)], axis=0
        )
        found = dot(picks.astype(F32).astype(BF16), table[...]).astype(BF16)
        for k in range(g, g + group):
            dy = order[k]
            block = found[(k - g) * cap : (k - g + 1) * cap]
            if dy == 0:
                fetched[y] = block
            else:
                reply[k] = block
                yy, _ = in_column(dy, 0)
                send(reply.at[k], fetched.at[y], 2, device(yy, z, x))

    for dy, dx in columns:
        if dx == 0:
            continue
        yy, xx = in_column(dy, dx)
        send(idx_own.at[yy], idx_all.at[x * ny + y], 1, device(yy, z, xx))

    loads[3].wait()
    loads[4].wait()
    loads[5].wait()
    dg = dot_nt(cot[...], w_out[...]).astype(BF16).astype(F32)
    bound = len_ref[:, :1]
    place_i = iota((tok, tok), 0)
    place_j = iota((tok, tok), 1)
    allowed = ((place_i >= bound) == (place_j >= bound)) & (place_j <= place_i)
    mask = jnp.where(allowed, 1.0 / MOST_LEN, 0.0).astype(F32)
    wait_recv(idx_all.at[pl.ds(0, (nx - 1) * ny)], 1)
    half_rows = shard_rows // nc
    for s in range(2):
        side = 1 - core if s == 0 else core
        m = iota((half_rows, cap), 0)
        row_at = (m // 16) * 32 + side * 16 + m % 16
        for k in range(nx * ny):
            hot[s, :, k * cap : (k + 1) * cap] = (
                (row_at == idx_all[k][:, :cap]).astype(F32).astype(BF16)
            )
    loads[6].wait()

    wait_recv(fetched.at[pl.ds(0, ny - 1)], 2)

    embedded = dot(unplace, fetched[...].reshape(slots, width)).astype(BF16)
    embedded = embedded.astype(F32)
    center = jnp.mean(embedded, axis=-1, keepdims=True)
    shifted = embedded - center
    scale = lax.rsqrt(jnp.mean(shifted * shifted, axis=-1, keepdims=True) + EPSILON)
    normed = shifted * scale
    normed_b = normed.astype(BF16)
    for i in range(4):
        hidden = dot(normed_b, w_in[:, i * width : (i + 1) * width])
        sig = sigmoid(hidden)
        value = hidden * sig
        branch[i] = value.astype(BF16)
        slope[i] = sig + value * (1.0 - sig)

    first_lane = iota((tok, pair_width), 1) < width // HEADS
    halves = [(0, tok // 2, tok // 2), (tok // 2, tok, tok)]

    def split(values):
        zero = jnp.zeros_like(values)
        return jnp.where(first_lane, values, zero), jnp.where(first_lane, zero, values)

    attended = []
    for p in range(pairs):
        lanes = slice(p * pair_width, (p + 1) * pair_width)
        v = split(branch[1, :, lanes])
        q = split(branch[2, :, lanes] * BF16(0.125))
        k = branch[3, :, lanes]
        result = []
        for lo, hi, js in halves:
            total = None
            for h in range(2):
                score = dot_nt(q[h][lo:hi], k[:js])
                sig = sigmoid(score)
                value = score * sig
                m = mask[lo:hi, :js]
                w = (value * m).astype(BF16)
                weight[2 * p + h, lo:hi, :js] = w
                sslope[2 * p + h, lo:hi, :js] = (sig + value * (1.0 - sig)) * m
                term = dot(w, v[h][:js])
                total = term if total is None else total + term
            result.append(total)
        attended.append(jnp.concatenate(result, axis=0))
    attended = jnp.concatenate(attended, axis=1)
    center2 = jnp.mean(attended, axis=-1, keepdims=True)
    shifted2 = attended - center2
    scale2 = lax.rsqrt(jnp.mean(shifted2 * shifted2, axis=-1, keepdims=True) + EPSILON)
    normed2 = shifted2 * scale2
    gate = branch[0].astype(F32)
    gated = (normed2 * gate).astype(BF16)

    wgrad = dot_tn(gated, cot[...])
    wgrad = [wgrad[:, c * half_width : (c + 1) * half_width] for c in range(2)]
    wsw_out[...] = jnp.where(core == 0, wgrad[1], wgrad[0]).astype(BF16)
    wown = jnp.where(core == 0, wgrad[0], wgrad[1])
    send(wsw_out, wsw_in, 3, sibling)

    out[...] = (dot(gated, w_out[...]) + embedded).astype(BF16)
    store = pltpu.make_async_copy(out, out_hbm, store_sem)
    store.start()

    d_n2 = dg * gate
    d_gate = (dg * normed2).astype(BF16).astype(F32)
    d_att = scale2 * (
        d_n2
        - jnp.mean(d_n2, axis=-1, keepdims=True)
        - normed2 * jnp.mean(d_n2 * normed2, axis=-1, keepdims=True)
    )
    d_att = d_att.astype(BF16)
    d_normed = dot_nt((d_gate * slope[0]).astype(BF16), w_in[:, :width])

    for p in range(pairs):
        lanes = slice(p * pair_width, (p + 1) * pair_width)
        if p == 1:
            wait_recv(wsw_in, 3)
            wblock = wown.shape[0] // (nz * nx)
            wrs_out[...] = (wown + wsw_in[...].astype(F32)).astype(BF16).reshape(nz * nx, wblock, half_width)
            wrs_in[zx] = wrs_out[zx]
            for dz, dx in planes:
                zz, xx = in_plane(dz, dx)
                send(wrs_out.at[zz * nx + xx], wrs_in.at[zx], 4, device(y, zz, xx))
        d_o = split(d_att[:, lanes])
        q = split(branch[2, :, lanes] * BF16(0.125))
        k = split(branch[3, :, lanes])
        v = branch[1, :, lanes]
        half = tok // 2
        dv_low = dv_all = dk_low = dk_all = None
        dq = []
        for lo, hi, js in halves:
            dq_sum = None
            for h in range(2):
                d_w = dot_nt(d_o[h][lo:hi], v[:js])
                d_s = (d_w * sslope[2 * p + h, lo:hi, :js]).astype(BF16)
                term = dot(d_s, k[h][:js])
                dq_sum = term if dq_sum is None else dq_sum + term
                dk = dot_tn(d_s, q[h][lo:hi])
                dv = dot_tn(weight[2 * p + h, lo:hi, :js], d_o[h][lo:hi])
                if lo == 0:
                    dk_low = dk if dk_low is None else dk_low + dk
                    dv_low = dv if dv_low is None else dv_low + dv
                else:
                    dk_all = dk if dk_all is None else dk_all + dk
                    dv_all = dv if dv_all is None else dv_all + dv
            dq.append(dq_sum * 0.125)
        dq = jnp.concatenate(dq, axis=0)
        dk = jnp.concatenate([dk_all[:half] + dk_low, dk_all[half:]], axis=0)
        dv = jnp.concatenate([dv_all[:half] + dv_low, dv_all[half:]], axis=0)
        for i, value in ((1, dv), (2, dq), (3, dk)):
            value = value.astype(BF16).astype(F32)
            sides[i - 1, :, lanes] = (value * slope[i, :, lanes]).astype(BF16)

    for i in range(1, 4):
        d_normed = d_normed + dot_nt(sides[i - 1], w_in[:, i * width : (i + 1) * width])
    d_normed = d_normed.astype(BF16).astype(F32)
    d_emb = scale * (
        d_normed
        - jnp.mean(d_normed, axis=-1, keepdims=True)
        - normed * jnp.mean(d_normed * normed, axis=-1, keepdims=True)
    )
    token_grads = (d_emb + cot[...].astype(F32)).astype(BF16)

    spread = dot(place[...], token_grads).astype(BF16)
    for xx in range(nx):
        packed[xx] = spread[:, xx * chunk : (xx + 1) * chunk].reshape(ny, cap, chunk)
    ret[x * ny + y] = packed[x, y]
    for dy, dx in columns:
        yy, xx = in_column(dy, dx)
        send(packed.at[xx, yy], ret.at[x * ny + y], 6, device(yy, z, xx))

    wait_recv(wrs_in.at[pl.ds(0, nz * nx - 1)], 4)
    wsum = jnp.sum(wrs_in[...].astype(F32), axis=0)
    way_out[...] = wsum.astype(BF16)

    wait_recv(ret.at[pl.ds(0, nx * ny - 1)], 6)
    way_in[y] = way_out[...]
    for dy in near:
        yy, _ = in_column(dy, 0)
        send(way_out, way_in.at[y], 5, device(yy, z, x))
    returned = ret[...].reshape(nx * slots, chunk)
    half_out[...] = dot(hot[0], returned).astype(BF16)
    send(half_out, half_in, 8, sibling)
    own_half = dot(hot[1], returned)
    wait_recv(half_in, 8)
    total = own_half + half_in[...].astype(F32)

    rs_out[...] = total.astype(BF16).reshape(nz * nx, 16, chunk)
    rs_in[zx] = rs_out[zx]
    for dz, dx in planes:
        zz, xx = in_plane(dz, dx)
        send(rs_out.at[zz * nx + xx], rs_in.at[zx], 9, device(y, zz, xx))

    wait_recv(way_in.at[pl.ds(0, ny - 1)], 5)
    wsum = jnp.sum(way_in[...].astype(F32), axis=0)
    wrows = wblock // nc
    wsum = [wsum[c * wrows : (c + 1) * wrows] for c in range(2)]
    wfin_out[...] = jnp.where(core == 0, wsum[1], wsum[0])
    wown = jnp.where(core == 0, wsum[0], wsum[1])
    send(wfin_out, wfin_in, 7, sibling)

    wait_recv(wfin_in, 7)
    wother = wfin_in[...]
    wgrad_ref[:, :half_width] = jnp.where(core == 0, wown, wother).astype(BF16)
    wgrad_ref[:, half_width:] = jnp.where(core == 0, wother, wown).astype(BF16)
    wait_send(idx_own.at[pl.ds(0, ny - 1)], 0)
    wait_send(idx_all.at[pl.ds(0, (nx - 1) * ny)], 1)
    wait_send(fetched.at[pl.ds(0, ny - 1)], 2)
    wait_send(wsw_out, 3)
    wait_send(wrs_out.at[pl.ds(0, nz * nx - 1)], 4)
    wait_send(way_in.at[pl.ds(0, ny - 1)], 5)
    wait_send(ret.at[pl.ds(0, nx * ny - 1)], 6)
    wait_send(wfin_out, 7)
    wait_send(half_out, 8)
    store.wait()
    wait_recv(rs_in.at[pl.ds(0, nz * nx - 1)], 9)
    for xx in range(nx):
        acc = None
        for zz in range(nz):
            term = rs_in[zz * nx + xx].astype(F32)
            acc = term if acc is None else acc + term
        tgrad_ref[:, xx * chunk : (xx + 1) * chunk] = acc
    wait_send(rs_out.at[pl.ds(0, nz * nx - 1)], 9)


def hand_on(*refs):
    sems = refs[-1]
    copies = [pltpu.make_async_copy(refs[i], refs[3 + i], sems.at[i]) for i in range(3)]
    for copy in copies:
        copy.start()
    for copy in copies:
        copy.wait()


def on_device(ny, nz, nx, cap, table, owner, local_row, lengths, w_in, w_out, cotangent):
    tok, width = cotangent.shape
    shard_rows = table.shape[0]
    chunk = width // nx
    slots = ny * cap
    nc = CORES
    wblock = width // (nz * nx)
    half_width = width // nc
    vmem = pl.BlockSpec(memory_space=pltpu.VMEM)
    anywhere = pl.BlockSpec(memory_space=pl.ANY)
    V = pltpu.VMEM
    scratch = [
        V((1, tok), jnp.int32),
        V((1, tok), jnp.int32),
        V(lengths.shape, jnp.int32),
        V(table.shape, BF16),
        V(w_in.shape, BF16),
        V(w_out.shape, BF16),
        V(cotangent.shape, BF16),
        V(cotangent.shape, BF16),
        V((ny, 1, -(-cap // 128) * 128), jnp.int32),
        V((nx * ny, 1, -(-cap // 128) * 128), jnp.int32),
        V((ny, cap, width), BF16),
        V((ny, cap, width), BF16),
        V((slots, tok), BF16),
        V((2, shard_rows // nc, nx * slots), BF16),
        V((4, tok, width), BF16),
        V((4, tok, width), F32),
        V((HEADS, tok, tok), BF16),
        V((HEADS, tok, tok), F32),
        V((3, tok, width), BF16),
        V((nx, ny, cap, chunk), BF16),
        V((nx * ny, cap, chunk), BF16),
        V((shard_rows // nc, chunk), BF16),
        V((shard_rows // nc, chunk), BF16),
        V((nz * nx, 16, chunk), BF16),
        V((nz * nx, 16, chunk), BF16),
        V((width, half_width), BF16),
        V((width, half_width), BF16),
        V((nz * nx, wblock, half_width), BF16),
        V((nz * nx, wblock, half_width), BF16),
        V((wblock, half_width), BF16),
        V((ny, wblock, half_width), BF16),
        V((wblock // nc, half_width), F32),
        V((wblock // nc, half_width), F32),
        pltpu.SemaphoreType.DMA((7,)),
        pltpu.SemaphoreType.DMA,
        pltpu.SemaphoreType.DMA((10,)),
        pltpu.SemaphoreType.DMA((10,)),
    ]
    results = pl.pallas_call(
        functools.partial(kernel, ny, nz, nx, cap),
        out_shape=(
            jax.ShapeDtypeStruct((tok, width), BF16),
            jax.ShapeDtypeStruct((shard_rows // (nz * nx * nc), width), F32),
            jax.ShapeDtypeStruct((wblock // nc, width), BF16),
        ),
        in_specs=[anywhere] * 7,
        out_specs=(anywhere, vmem, vmem),
        scratch_shapes=scratch,
        compiler_params=pltpu.CompilerParams(
            collective_id=0, has_side_effects=True, vmem_limit_bytes=56 * 1024 * 1024
        ),
        name="hstu",
    )(
        owner.reshape(1, tok),
        local_row.reshape(1, tok),
        lengths,
        table,
        w_in,
        w_out,
        cotangent,
    )
    return pl.pallas_call(
        hand_on,
        out_shape=tuple(jax.ShapeDtypeStruct(r.shape, r.dtype) for r in results),
        in_specs=[anywhere] * 3,
        out_specs=(anywhere,) * 3,
        scratch_shapes=[pltpu.SemaphoreType.DMA((3,))],
        name="hand_on",
    )(*results)


def build(mesh, nx, cap):
    ny = mesh.shape["table"]
    nz = mesh.shape["batch"] // (nx * CORES)
    return jax.shard_map(
        functools.partial(on_device, ny, nz, nx, cap),
        mesh=mesh,
        in_specs=(
            P("table", None),
            P(("table", "batch"), None),
            P(("table", "batch")),
            P(("table", "batch"), None),
            P(),
            P(),
            P(("table", "batch"), None),
        ),
        out_specs=(P(("table", "batch"), None), P(("table", "batch"), None), P("batch", None)),
        check_vma=False,
    )


def solution(mesh):
    return build(mesh, 4, 48)
```

time: 301 us -> 78.9 us (0.26); the launches traced: 295 us -> 78.8 us
  blocking collectives: 127 us -> 0 us
  Pallas kernels: 0 us -> 78.1 us
  local copies, waits for them, and re-layouts: 65.3 us -> 0 us
  waiting for transfers between devices: 51 us -> 0 us
  matrix products: 17.5 us -> 0 us
  between operations: 14.4 us -> 0.64 us
  other arithmetic: 12.5 us -> 0 us
  starting transfers between devices: 7.38 us -> 0 us
    psum x1 -> x0, blocking collectives: 113 us -> none  [on_device(): summed = lax.psum(local_term, ('table', 'batch'))]
    pallas_call x0 -> x2, Pallas kernels: none -> 78.1 us  [the longest x1 67.8 us: on_device(): pl.pallas_call(functools.partial(kernel, ny, nz, nx, cap), out_shape=(jax...]
    scatter x2 -> x0, local copies, waits for them, and re-layouts: 54.4 us -> none  [the longest x1 33 us: on_device(): jnp.zeros((shard_count, capacity, width), jnp.bfloat16).at[column, rank]]
    reduce_scatter x1 -> x0, waiting for transfers between devices: 31.5 us -> none  [on_device(): lax.psum_scatter(dense, 'batch', scatter_dimension=0, tiled=True)]
    all_to_all x2 -> x0, waiting for transfers between devices: 19.5 us -> none  [the longest x1 10.3 us: on_device(): lax.all_to_all(replies, 'table', split_axis=0, concat_axis=0, tiled=True)]
    dot_general x11 -> x0, matrix products: 17.5 us -> none  [the longest x2 4.96 us: hstu_block(): hidden = jnp.dot(normed, w_in, preferred_element_type=jnp.float32)]
    all_to_all x1 -> x0, blocking collectives: 14 us -> none  [on_device(): lax.all_to_all(requests, 'table', split_axis=0, concat_axis=0, tiled=True)]
    all_to_all x2 -> x0, starting transfers between devices: 7.16 us -> none  [the longest x1 3.71 us: on_device(): lax.all_to_all(grad_slots, 'table', split_axis=0, concat_axis=0, tiled=True)]
  transfers between devices with their start and end apart: 3 -> 0, of which waited for: 3 -> 0; matrix products, arithmetic and copies ran while one was open for 2% -> 0% of each run, Pallas kernels for 0% -> 0%
where the time goes in v1:
time: 78.9 us; the launch traced here: 78.8 us
  Pallas kernels  78.1 us (99%)
    pallas_call x1, Pallas kernels, on_device(): pl.pallas_call(functools.partial(kernel, ny, nz, nx, cap), out_shape=(jax...  67.8 us
    pallas_call x1, Pallas kernels, on_device(): pl.pallas_call(hand_on, out_shape=tuple((jax.ShapeDtypeStruct(r.shape, r....  10.3 us

profile of v1, /device:TPU:1, one launch (start us, length us, event | category | flops | bytes accessed | tf_op | source)
XLA Modules:
  0.0 78.8 jit_solution(10140009190121461884)
XLA Ops:
  0.6 67.8 %hstu.1 = (bf16[256,512]{1,0:T(8,128)(2,1)}, f32[16,512]{1,0:T(8,128)}, bf16[8,512]{1,0:T(8,128)(2,1)}) custom-call(s32[1,256]{1,0:T(1,128)} %bitcast.2, s32[1,256]{1,0:T(1,128)} %bitcast.3, s32[1,2]{1,0:T(1,128)} %len_hbm.1, bf16[1024,512]{1,0:T(8,128)(2,1)} %table_hbm.1, bf16[512,2048]{1,0:T(8,128)(2,1)} %w_in_hbm.1, bf16[512,512]{1,0:T(8,128)(2,1)} %w_out_hbm.1, ...), custom_call_target="tpu_custom_call" | custom-call | tf_op jit(solution)/shard_map/hstu/pallas_call | solution.py:452
  68.5 10.3 %hand_on.1 = (bf16[256,512]{1,0:T(8,128)(2,1)}, f32[16,512]{1,0:T(8,128)}, bf16[8,512]{1,0:T(8,128)(2,1)}) custom-call(bf16[256,512]{1,0:T(8,128)(2,1)} %get-tuple-element.6.refs_0_, f32[16,512]{1,0:T(8,128)} %get-tuple-element.7.refs_1_, bf16[8,512]{1,0:T(8,128)(2,1)} %get-tuple-element.8.refs_2_), custom_call_target="tpu_custom_call" | custom-call | tf_op jit(solution)/shard_map/hand_on/pallas_call | solution.py:475

commit v2 on v1

--- a/solution.py
+++ b/solution.py
@@ -194,16 +194,6 @@
     place_j = iota((tok, tok), 1)
     allowed = ((place_i >= bound) == (place_j >= bound)) & (place_j <= place_i)
     mask = jnp.where(allowed, 1.0 / MOST_LEN, 0.0).astype(F32)
-    wait_recv(idx_all.at[pl.ds(0, (nx - 1) * ny)], 1)
-    half_rows = shard_rows // nc
-    for s in range(2):
-        side = 1 - core if s == 0 else core
-        m = iota((half_rows, cap), 0)
-        row_at = (m // 16) * 32 + side * 16 + m % 16
-        for k in range(nx * ny):
-            hot[s, :, k * cap : (k + 1) * cap] = (
-                (row_at == idx_all[k][:, :cap]).astype(F32).astype(BF16)
-            )
     loads[6].wait()
 
     wait_recv(fetched.at[pl.ds(0, ny - 1)], 2)
@@ -280,14 +270,6 @@
 
     for p in range(pairs):
         lanes = slice(p * pair_width, (p + 1) * pair_width)
-        if p == 1:
-            wait_recv(wsw_in, 3)
-            wblock = wown.shape[0] // (nz * nx)
-            wrs_out[...] = (wown + wsw_in[...].astype(F32)).astype(BF16).reshape(nz * nx, wblock, half_width)
-            wrs_in[zx] = wrs_out[zx]
-            for dz, dx in planes:
-                zz, xx = in_plane(dz, dx)
-                send(wrs_out.at[zz * nx + xx], wrs_in.at[zx], 4, device(y, zz, xx))
         d_o = split(d_att[:, lanes])
         q = split(branch[2, :, lanes] * BF16(0.125))
         k = split(branch[3, :, lanes])
@@ -336,6 +318,25 @@
         yy, xx = in_column(dy, dx)
         send(packed.at[xx, yy], ret.at[x * ny + y], 6, device(yy, z, xx))
 
+    wait_recv(wsw_in, 3)
+    wblock = wown.shape[0] // (nz * nx)
+    wrs_out[...] = (wown + wsw_in[...].astype(F32)).astype(BF16).reshape(nz * nx, wblock, half_width)
+    wrs_in[zx] = wrs_out[zx]
+    for dz, dx in planes:
+        zz, xx = in_plane(dz, dx)
+        send(wrs_out.at[zz * nx + xx], wrs_in.at[zx], 4, device(y, zz, xx))
+
+    wait_recv(idx_all.at[pl.ds(0, (nx - 1) * ny)], 1)
+    half_rows = shard_rows // nc
+    for s in range(2):
+        side = 1 - core if s == 0 else core
+        m = iota((half_rows, cap), 0)
+        row_at = (m // 16) * 32 + side * 16 + m % 16
+        for k in range(nx * ny):
+            hot[s, :, k * cap : (k + 1) * cap] = (
+                (row_at == idx_all[k][:, :cap]).astype(F32).astype(BF16)
+            )
+
     wait_recv(wrs_in.at[pl.ds(0, nz * nx - 1)], 4)
     wsum = jnp.sum(wrs_in[...].astype(F32), axis=0)
     way_out[...] = wsum.astype(BF16)
@@ -391,12 +392,8 @@
 
 
 def hand_on(*refs):
-    sems = refs[-1]
-    copies = [pltpu.make_async_copy(refs[i], refs[3 + i], sems.at[i]) for i in range(3)]
-    for copy in copies:
-        copy.start()
-    for copy in copies:
-        copy.wait()
+    for i in range(3):
+        refs[3 + i][...] = refs[i][...]
 
 
 def on_device(ny, nz, nx, cap, table, owner, local_row, lengths, w_in, w_out, cotangent):
@@ -475,9 +472,8 @@
     return pl.pallas_call(
         hand_on,
         out_shape=tuple(jax.ShapeDtypeStruct(r.shape, r.dtype) for r in results),
-        in_specs=[anywhere] * 3,
-        out_specs=(anywhere,) * 3,
-        scratch_shapes=[pltpu.SemaphoreType.DMA((3,))],
+        in_specs=[vmem] * 3,
+        out_specs=(vmem,) * 3,
         name="hand_on",
     )(*results)
 

time: 78.9 us -> 61.4 us (0.78)
  Pallas kernels: 78.1 us -> 60.7 us
    pallas_call x1, Pallas kernels: 67.8 us -> 59 us  [on_device(): pl.pallas_call(functools.partial(kernel, ny, nz, nx, cap), out_shape=(jax...]
    pallas_call x1, Pallas kernels: 10.3 us -> 1.7 us  [on_device(): pl.pallas_call(hand_on, out_shape=tuple((jax.ShapeDtypeStruct(r.shape, r....]
where the time goes in v2:
time: 61.4 us; the launch traced here: 61.3 us
  Pallas kernels  60.7 us (99%)
  between operations  0.64 us (1%)
    pallas_call x1, Pallas kernels, on_device(): pl.pallas_call(functools.partial(kernel, ny, nz, nx, cap), out_shape=(jax...  59 us
    pallas_call x1, Pallas kernels, on_device(): pl.pallas_call(hand_on, out_shape=tuple((jax.ShapeDtypeStruct(r.shape, r....  1.7 us

profile of v2, /device:TPU:1, one launch (start us, length us, event | category | flops | bytes accessed | tf_op | source)
XLA Modules:
  0.0 61.3 jit_solution(17690882809700044392)
XLA Ops:
  0.6 59.0 %hstu.1 = (bf16[256,512]{1,0:T(8,128)(2,1)}, f32[16,512]{1,0:T(8,128)}, bf16[8,512]{1,0:T(8,128)(2,1)}) custom-call(s32[1,256]{1,0:T(1,128)} %bitcast.2, s32[1,256]{1,0:T(1,128)} %bitcast.3, s32[1,2]{1,0:T(1,128)} %len_hbm.1, bf16[1024,512]{1,0:T(8,128)(2,1)} %table_hbm.1, bf16[512,2048]{1,0:T(8,128)(2,1)} %w_in_hbm.1, bf16[512,512]{1,0:T(8,128)(2,1)} %w_out_hbm.1, ...), custom_call_target="tpu_custom_call" | custom-call | tf_op jit(solution)/shard_map/hstu/pallas_call | solution.py:449
  59.6 1.7 %hand_on.1 = (bf16[256,512]{1,0:T(8,128)(2,1)}, f32[16,512]{1,0:T(8,128)}, bf16[8,512]{1,0:T(8,128)(2,1)}) custom-call(bf16[256,512]{1,0:T(8,128)(2,1)} %get-tuple-element.6.refs_0_, f32[16,512]{1,0:T(8,128)} %get-tuple-element.7.refs_1_, bf16[8,512]{1,0:T(8,128)(2,1)} %get-tuple-element.8.refs_2_), custom_call_target="tpu_custom_call" | custom-call | tf_op jit(solution)/shard_map/hand_on/pallas_call | solution.py:472

commit v3 on v2

--- a/solution.py
+++ b/solution.py
@@ -72,6 +72,8 @@
     columns = [(dy, dx) for dy in far_first(ny) for dx in far_first(nx) if (dy, dx) != (0, 0)]
     planes = [(dz, dx) for dz in far_first(nz) for dx in far_first(nx) if (dz, dx) != (0, 0)]
 
+    own_column, own_plane = len(columns), len(planes)
+
     def in_column(dy, dx):
         return (y + dy) & (ny - 1), (x + dx) & (nx - 1)
 
@@ -80,15 +82,13 @@
 
     barrier = pltpu.get_barrier_semaphore()
     greeted = 0
-    for dy, dx in columns:
-        yy, xx = in_column(dy, dx)
-        pl.semaphore_signal(barrier, inc=1, device_id=device(yy, z, xx))
-        greeted += 1
-    for dz, dx in planes:
-        if dz == 0:
-            continue
-        zz, xx = in_plane(dz, dx)
-        pl.semaphore_signal(barrier, inc=1, device_id=device(y, zz, xx))
+    axes = (
+        [device((y + d) & (ny - 1), z, x) for d in far_first(ny) if d]
+        + [device(y, (z + d) & (nz - 1), x) for d in far_first(nz) if d]
+        + [device(y, z, (x + d) & (nx - 1)) for d in far_first(nx) if d]
+    )
+    for target in axes:
+        pl.semaphore_signal(barrier, inc=1, device_id=target)
         greeted += 1
     pl.semaphore_signal(barrier, inc=1, device_id=sibling)
     greeted += 1
@@ -126,7 +126,7 @@
     listed = (listed[:ny] * 32.0 + listed[ny:]).astype(jnp.int32)
     for o in range(ny):
         idx_own[o] = listed[o : o + 1]
-    idx_all[x * ny + y] = idx_own[y]
+    idx_all[own_column] = idx_own[y]
     slot = owner * cap + rank
     place[...] = (iota((slots, tok), 0) == slot).astype(F32).astype(BF16)
     slot_col = jnp.broadcast_to(slot.astype(F32), (8, tok)).T[:, :1].astype(jnp.int32)
@@ -153,12 +153,12 @@
     near = [dy for dy in far_first(ny) if dy]
     for dy in near:
         yy, _ = in_column(dy, 0)
-        send(idx_own.at[yy], idx_all.at[x * ny + y], 0, device(yy, z, x))
+        send(idx_own.at[yy], idx_all.at[columns.index((dy, 0))], 0, device(yy, z, x))
     loads[2].wait()
     wait_recv(idx_all.at[pl.ds(0, ny - 1)], 0)
 
     order = far_first(ny)
-    asked = [idx_all[x * ny + ((y + dy) & (ny - 1))] for dy in order]
+    asked = [idx_all[columns.index((dy, 0)) if dy else own_column] for dy in order]
     if ny < 8:
         asked = asked + [asked[0]] * (8 - ny)
     asked = jnp.concatenate(asked, axis=0).astype(F32).T.astype(jnp.int32)
@@ -176,14 +176,13 @@
                 fetched[y] = block
             else:
                 reply[k] = block
-                yy, _ = in_column(dy, 0)
+                yy, _ = in_column(-dy, 0)
                 send(reply.at[k], fetched.at[y], 2, device(yy, z, x))
 
-    for dy, dx in columns:
-        if dx == 0:
-            continue
-        yy, xx = in_column(dy, dx)
-        send(idx_own.at[yy], idx_all.at[x * ny + y], 1, device(yy, z, xx))
+    for j, (dy, dx) in enumerate(columns):
+        if dx:
+            yy, xx = in_column(dy, dx)
+            send(idx_own.at[yy], idx_all.at[j], 1, device(yy, z, xx))
 
     loads[3].wait()
     loads[4].wait()
@@ -310,14 +309,19 @@
     )
     token_grads = (d_emb + cot[...].astype(F32)).astype(BF16)
 
+    parts_of = 4 if nx * ny >= 8 else 2
+    part = nx * ny // parts_of
+    last = parts_of - 1
+    arrivals = 10
     spread = dot(place[...], token_grads).astype(BF16)
     for xx in range(nx):
         packed[xx] = spread[:, xx * chunk : (xx + 1) * chunk].reshape(ny, cap, chunk)
-    ret[x * ny + y] = packed[x, y]
-    for dy, dx in columns:
+    ret[own_column] = packed[x, y]
+    for j, (dy, dx) in enumerate(columns):
         yy, xx = in_column(dy, dx)
-        send(packed.at[xx, yy], ret.at[x * ny + y], 6, device(yy, z, xx))
-
+        send(packed.at[xx, yy], ret.at[j], arrivals + j // part, device(yy, z, xx))
+
+    wait_recv(idx_all.at[pl.ds(0, (nx - 1) * ny)], 1)
     wait_recv(wsw_in, 3)
     wblock = wown.shape[0] // (nz * nx)
     wrs_out[...] = (wown + wsw_in[...].astype(F32)).astype(BF16).reshape(nz * nx, wblock, half_width)
@@ -326,38 +330,54 @@
         zz, xx = in_plane(dz, dx)
         send(wrs_out.at[zz * nx + xx], wrs_in.at[zx], 4, device(y, zz, xx))
 
-    wait_recv(idx_all.at[pl.ds(0, (nx - 1) * ny)], 1)
     half_rows = shard_rows // nc
+    m = iota((16, nx * slots), 0)
+    starts = [(z_ * nx + x_) * 32 for z_, x_ in [in_plane(*d) for d in planes + [(0, 0)]]]
+    listed = jnp.concatenate([idx_all[j][:, :cap] for j in range(nx * ny)], axis=1)
     for s in range(2):
         side = 1 - core if s == 0 else core
-        m = iota((half_rows, cap), 0)
-        row_at = (m // 16) * 32 + side * 16 + m % 16
-        for k in range(nx * ny):
-            hot[s, :, k * cap : (k + 1) * cap] = (
-                (row_at == idx_all[k][:, :cap]).astype(F32).astype(BF16)
+        for g, start in enumerate(starts):
+            hot[s, g * 16 : (g + 1) * 16] = (
+                (m + (start + side * 16) == listed).astype(F32).astype(BF16)
             )
+
+    sums = [None, None]
+    for a in range(last):
+        wait_recv(ret.at[pl.ds(0, part)], arrivals + a)
+        block = ret[a * part : (a + 1) * part].reshape(part * cap, chunk)
+        for s in range(2):
+            term = dot(hot[s, :, a * part * cap : (a + 1) * part * cap], block)
+            sums[s] = term if a == 0 else sums[s] + term
 
     wait_recv(wrs_in.at[pl.ds(0, nz * nx - 1)], 4)
     wsum = jnp.sum(wrs_in[...].astype(F32), axis=0)
     way_out[...] = wsum.astype(BF16)
 
-    wait_recv(ret.at[pl.ds(0, nx * ny - 1)], 6)
+    wait_recv(ret.at[pl.ds(0, part - 1)], arrivals + last)
+    block = ret[last * part :].reshape(part * cap, chunk)
+    pieces = [slice(0, half_rows // 2), slice(half_rows // 2, half_rows)]
+
+    def piece_sum(s, piece):
+        return sums[s][piece] + dot(hot[s, piece, last * part * cap :], block)
+
+    for stage, piece in zip((6, 8), pieces):
+        half_out[piece] = piece_sum(0, piece).astype(BF16)
+        send(half_out.at[piece], half_in.at[piece], stage, sibling)
     way_in[y] = way_out[...]
     for dy in near:
         yy, _ = in_column(dy, 0)
         send(way_out, way_in.at[y], 5, device(yy, z, x))
-    returned = ret[...].reshape(nx * slots, chunk)
-    half_out[...] = dot(hot[0], returned).astype(BF16)
-    send(half_out, half_in, 8, sibling)
-    own_half = dot(hot[1], returned)
-    wait_recv(half_in, 8)
-    total = own_half + half_in[...].astype(F32)
-
-    rs_out[...] = total.astype(BF16).reshape(nz * nx, 16, chunk)
-    rs_in[zx] = rs_out[zx]
-    for dz, dx in planes:
-        zz, xx = in_plane(dz, dx)
-        send(rs_out.at[zz * nx + xx], rs_in.at[zx], 9, device(y, zz, xx))
+    own = [piece_sum(1, piece) for piece in pieces]
+
+    groups = nz * nx // 2
+    for i, (stage, piece) in enumerate(zip((6, 8), pieces)):
+        wait_recv(half_in.at[piece], stage)
+        total = own[i] + half_in[piece].astype(F32)
+        rs_out[i * groups : (i + 1) * groups] = total.astype(BF16).reshape(groups, 16, chunk)
+        for g in range(i * groups, min((i + 1) * groups, own_plane)):
+            zz, xx = in_plane(*planes[g])
+            send(rs_out.at[g], rs_in.at[g], 9, device(y, zz, xx))
+    rs_in[own_plane] = rs_out[own_plane]
 
     wait_recv(way_in.at[pl.ds(0, ny - 1)], 5)
     wsum = jnp.sum(way_in[...].astype(F32), axis=0)
@@ -377,23 +397,36 @@
     wait_send(wsw_out, 3)
     wait_send(wrs_out.at[pl.ds(0, nz * nx - 1)], 4)
     wait_send(way_in.at[pl.ds(0, ny - 1)], 5)
-    wait_send(ret.at[pl.ds(0, nx * ny - 1)], 6)
+    for a in range(parts_of):
+        wait_send(ret.at[pl.ds(0, part - (a == last))], arrivals + a)
     wait_send(wfin_out, 7)
-    wait_send(half_out, 8)
+    for stage, piece in zip((6, 8), pieces):
+        wait_send(half_out.at[piece], stage)
     store.wait()
     wait_recv(rs_in.at[pl.ds(0, nz * nx - 1)], 9)
-    for xx in range(nx):
+    for dx in range(nx):
         acc = None
-        for zz in range(nz):
-            term = rs_in[zz * nx + xx].astype(F32)
-            acc = term if acc is None else acc + term
-        tgrad_ref[:, xx * chunk : (xx + 1) * chunk] = acc
+        for g, (dz, dx_) in enumerate(planes + [(0, 0)]):
+            if dx_ == dx:
+                term = rs_in[g].astype(F32)
+                acc = term if acc is None else acc + term
+        start = pl.multiple_of(((x - dx) & (nx - 1)) * chunk, chunk)
+        tgrad_ref[:, pl.ds(start, chunk)] = acc
     wait_send(rs_out.at[pl.ds(0, nz * nx - 1)], 9)
 
 
 def hand_on(*refs):
+    given, results, held = refs[:3], refs[3:6], refs[6:9]
+    in_sem, out_sem = refs[9:]
+    ins = [pltpu.make_async_copy(given[i], held[i], in_sem.at[i]) for i in range(3)]
+    outs = [pltpu.make_async_copy(held[i], results[i], out_sem.at[i]) for i in range(3)]
+    for copy in ins:
+        copy.start()
     for i in range(3):
-        refs[3 + i][...] = refs[i][...]
+        ins[i].wait()
+        outs[i].start()
+    for copy in outs:
+        copy.wait()
 
 
 def on_device(ny, nz, nx, cap, table, owner, local_row, lengths, w_in, w_out, cotangent):
@@ -443,8 +476,8 @@
         V((wblock // nc, half_width), F32),
         pltpu.SemaphoreType.DMA((7,)),
         pltpu.SemaphoreType.DMA,
-        pltpu.SemaphoreType.DMA((10,)),
-        pltpu.SemaphoreType.DMA((10,)),
+        pltpu.SemaphoreType.DMA((14,)),
+        pltpu.SemaphoreType.DMA((14,)),
     ]
     results = pl.pallas_call(
         functools.partial(kernel, ny, nz, nx, cap),
@@ -457,7 +490,7 @@
         out_specs=(anywhere, vmem, vmem),
         scratch_shapes=scratch,
         compiler_params=pltpu.CompilerParams(
-            collective_id=0, has_side_effects=True, vmem_limit_bytes=56 * 1024 * 1024
+            collective_id=0, has_side_effects=True, fuse_transposed_lhs_in_matmul=True, vmem_limit_bytes=56 * 1024 * 1024
         ),
         name="hstu",
     )(
@@ -472,8 +505,10 @@
     return pl.pallas_call(
         hand_on,
         out_shape=tuple(jax.ShapeDtypeStruct(r.shape, r.dtype) for r in results),
-        in_specs=[vmem] * 3,
-        out_specs=(vmem,) * 3,
+        in_specs=[anywhere] * 3,
+        out_specs=(anywhere,) * 3,
+        scratch_shapes=[V(r.shape, r.dtype) for r in results]
+        + [pltpu.SemaphoreType.DMA((3,)), pltpu.SemaphoreType.DMA((3,))],
         name="hand_on",
     )(*results)
 

time: 61.4 us -> 58.5 us (0.953)
  Pallas kernels: 60.7 us -> 57.7 us
    pallas_call x1, Pallas kernels: 59 us -> 56 us  [on_device(): pl.pallas_call(functools.partial(kernel, ny, nz, nx, cap), out_shape=(jax...]
where the time goes in v3:
time: 58.5 us; the launch traced here: 58.4 us
  Pallas kernels  57.7 us (99%)
  between operations  0.64 us (1%)
    pallas_call x1, Pallas kernels, on_device(): pl.pallas_call(functools.partial(kernel, ny, nz, nx, cap), out_shape=(jax...  56 us
    pallas_call x1, Pallas kernels, on_device(): pl.pallas_call(hand_on, out_shape=tuple((jax.ShapeDtypeStruct(r.shape, r....  1.71 us

profile of v3, /device:TPU:1, one launch (start us, length us, event | category | flops | bytes accessed | tf_op | source)
XLA Modules:
  0.0 58.4 jit_solution(6613284354436249087)
XLA Ops:
  0.6 56.0 %hstu.1 = (bf16[256,512]{1,0:T(8,128)(2,1)}, f32[16,512]{1,0:T(8,128)}, bf16[8,512]{1,0:T(8,128)(2,1)}) custom-call(s32[1,256]{1,0:T(1,128)} %bitcast.2, s32[1,256]{1,0:T(1,128)} %bitcast.3, s32[1,2]{1,0:T(1,128)} %len_hbm.1, bf16[1024,512]{1,0:T(8,128)(2,1)} %table_hbm.1, bf16[512,2048]{1,0:T(8,128)(2,1)} %w_in_hbm.1, bf16[512,512]{1,0:T(8,128)(2,1)} %w_out_hbm.1, ...), custom_call_target="tpu_custom_call" | custom-call | tf_op jit(solution)/shard_map/hstu/pallas_call | solution.py:482
  56.7 1.7 %hand_on.1 = (bf16[256,512]{1,0:T(8,128)(2,1)}, f32[16,512]{1,0:T(8,128)}, bf16[8,512]{1,0:T(8,128)(2,1)}) custom-call(bf16[256,512]{1,0:T(8,128)(2,1)} %get-tuple-element.6.refs_0_, f32[16,512]{1,0:T(8,128)} %get-tuple-element.7.refs_1_, bf16[8,512]{1,0:T(8,128)(2,1)} %get-tuple-element.8.refs_2_), custom_call_target="tpu_custom_call" | custom-call | tf_op jit(solution)/shard_map/hand_on/pallas_call | solution.py:505

commit v4 on v3

--- a/solution.py
+++ b/solution.py
@@ -151,33 +151,34 @@
         pltpu.make_async_copy(slab, slab, send_sem.at[stage]).wait()
 
     near = [dy for dy in far_first(ny) if dy]
+    lists = 13
     for dy in near:
         yy, _ = in_column(dy, 0)
-        send(idx_own.at[yy], idx_all.at[columns.index((dy, 0))], 0, device(yy, z, x))
+        send(idx_own.at[yy], idx_all.at[columns.index((dy, 0))], lists + dy, device(yy, z, x))
     loads[2].wait()
-    wait_recv(idx_all.at[pl.ds(0, ny - 1)], 0)
-
-    order = far_first(ny)
-    asked = [idx_all[columns.index((dy, 0)) if dy else own_column] for dy in order]
-    if ny < 8:
-        asked = asked + [asked[0]] * (8 - ny)
-    asked = jnp.concatenate(asked, axis=0).astype(F32).T.astype(jnp.int32)
+
+    order = near[::-1] + [0]
     shard_rows = table.shape[0]
     group = 2
-    for g in range(0, ny, group):
+    for first in range(0, ny, group):
+        turn = order[first : first + group]
+        for dy in turn:
+            if dy:
+                wait_recv(idx_all.at[pl.ds(0, 1)], lists + dy)
+        asked = [idx_all[columns.index((dy, 0)) if dy else own_column] for dy in turn]
+        asked = jnp.concatenate(asked * (8 // group), axis=0).astype(F32).T.astype(jnp.int32)
         picks = jnp.concatenate(
-            [iota((cap, shard_rows), 1) == asked[:cap, k : k + 1] for k in range(g, g + group)], axis=0
+            [iota((cap, shard_rows), 1) == asked[:cap, k : k + 1] for k in range(group)], axis=0
         )
         found = dot(picks.astype(F32).astype(BF16), table[...]).astype(BF16)
-        for k in range(g, g + group):
-            dy = order[k]
-            block = found[(k - g) * cap : (k - g + 1) * cap]
+        for k, dy in enumerate(turn):
+            block = found[k * cap : (k + 1) * cap]
             if dy == 0:
                 fetched[y] = block
             else:
-                reply[k] = block
+                reply[dy] = block
                 yy, _ = in_column(-dy, 0)
-                send(reply.at[k], fetched.at[y], 2, device(yy, z, x))
+                send(reply.at[dy], fetched.at[y], 2, device(yy, z, x))
 
     for j, (dy, dx) in enumerate(columns):
         if dx:
@@ -391,7 +392,8 @@
     wother = wfin_in[...]
     wgrad_ref[:, :half_width] = jnp.where(core == 0, wown, wother).astype(BF16)
     wgrad_ref[:, half_width:] = jnp.where(core == 0, wother, wown).astype(BF16)
-    wait_send(idx_own.at[pl.ds(0, ny - 1)], 0)
+    for dy in near:
+        wait_send(idx_own.at[pl.ds(0, 1)], lists + dy)
     wait_send(idx_all.at[pl.ds(0, (nx - 1) * ny)], 1)
     wait_send(fetched.at[pl.ds(0, ny - 1)], 2)
     wait_send(wsw_out, 3)
@@ -476,8 +478,8 @@
         V((wblock // nc, half_width), F32),
         pltpu.SemaphoreType.DMA((7,)),
         pltpu.SemaphoreType.DMA,
-        pltpu.SemaphoreType.DMA((14,)),
-        pltpu.SemaphoreType.DMA((14,)),
+        pltpu.SemaphoreType.DMA((13 + ny,)),
+        pltpu.SemaphoreType.DMA((13 + ny,)),
     ]
     results = pl.pallas_call(
         functools.partial(kernel, ny, nz, nx, cap),

time: 58.5 us -> 57.4 us (0.981)
  Pallas kernels: 57.7 us -> 56.7 us
    pallas_call x1, Pallas kernels: 56 us -> 54.9 us  [on_device(): pl.pallas_call(functools.partial(kernel, ny, nz, nx, cap), out_shape=(jax...]
where the time goes in v4:
time: 57.4 us; the launch traced here: 57.3 us
  Pallas kernels  56.7 us (99%)
  between operations  0.64 us (1%)
    pallas_call x1, Pallas kernels, on_device(): pl.pallas_call(functools.partial(kernel, ny, nz, nx, cap), out_shape=(jax...  54.9 us
    pallas_call x1, Pallas kernels, on_device(): pl.pallas_call(hand_on, out_shape=tuple((jax.ShapeDtypeStruct(r.shape, r....  1.71 us

profile of v4, /device:TPU:1, one launch (start us, length us, event | category | flops | bytes accessed | tf_op | source)
XLA Modules:
  0.0 57.3 jit_solution(4318771472600211295)
XLA Ops:
  0.6 54.9 %hstu.1 = (bf16[256,512]{1,0:T(8,128)(2,1)}, f32[16,512]{1,0:T(8,128)}, bf16[8,512]{1,0:T(8,128)(2,1)}) custom-call(s32[1,256]{1,0:T(1,128)} %bitcast.2, s32[1,256]{1,0:T(1,128)} %bitcast.3, s32[1,2]{1,0:T(1,128)} %len_hbm.1, bf16[1024,512]{1,0:T(8,128)(2,1)} %table_hbm.1, bf16[512,2048]{1,0:T(8,128)(2,1)} %w_in_hbm.1, bf16[512,512]{1,0:T(8,128)(2,1)} %w_out_hbm.1, ...), custom_call_target="tpu_custom_call" | custom-call | tf_op jit(solution)/shard_map/hstu/pallas_call | solution.py:484
  55.6 1.7 %hand_on.1 = (bf16[256,512]{1,0:T(8,128)(2,1)}, f32[16,512]{1,0:T(8,128)}, bf16[8,512]{1,0:T(8,128)(2,1)}) custom-call(bf16[256,512]{1,0:T(8,128)(2,1)} %get-tuple-element.6.refs_0_, f32[16,512]{1,0:T(8,128)} %get-tuple-element.7.refs_1_, bf16[8,512]{1,0:T(8,128)(2,1)} %get-tuple-element.8.refs_2_), custom_call_target="tpu_custom_call" | custom-call | tf_op jit(solution)/shard_map/hand_on/pallas_call | solution.py:507

commit v5 on v4

--- a/solution.py
+++ b/solution.py
@@ -80,19 +80,6 @@
     def in_plane(dz, dx):
         return (z + dz) & (nz - 1), (x + dx) & (nx - 1)
 
-    barrier = pltpu.get_barrier_semaphore()
-    greeted = 0
-    axes = (
-        [device((y + d) & (ny - 1), z, x) for d in far_first(ny) if d]
-        + [device(y, (z + d) & (nz - 1), x) for d in far_first(nz) if d]
-        + [device(y, z, (x + d) & (nx - 1)) for d in far_first(nx) if d]
-    )
-    for target in axes:
-        pl.semaphore_signal(barrier, inc=1, device_id=target)
-        greeted += 1
-    pl.semaphore_signal(barrier, inc=1, device_id=sibling)
-    greeted += 1
-
     loads = [
         pltpu.make_async_copy(src, dst, load_sem.at[i])
         for i, (src, dst) in enumerate(
@@ -107,7 +94,23 @@
             ]
         )
     ]
-    for load in loads:
+    for load in loads[:2]:
+        load.start()
+
+    barrier = pltpu.get_barrier_semaphore()
+    greeted = 0
+    axes = (
+        [device((y + d) & (ny - 1), z, x) for d in far_first(ny) if d]
+        + [device(y, (z + d) & (nz - 1), x) for d in far_first(nz) if d]
+        + [device(y, z, (x + d) & (nx - 1)) for d in far_first(nx) if d]
+    )
+    for target in axes:
+        pl.semaphore_signal(barrier, inc=1, device_id=target)
+        greeted += 1
+    pl.semaphore_signal(barrier, inc=1, device_id=sibling)
+    greeted += 1
+
+    for load in loads[2:]:
         load.start()
 
     loads[0].wait()
@@ -127,10 +130,6 @@
     for o in range(ny):
         idx_own[o] = listed[o : o + 1]
     idx_all[own_column] = idx_own[y]
-    slot = owner * cap + rank
-    place[...] = (iota((slots, tok), 0) == slot).astype(F32).astype(BF16)
-    slot_col = jnp.broadcast_to(slot.astype(F32), (8, tok)).T[:, :1].astype(jnp.int32)
-    unplace = (iota((tok, slots), 1) == slot_col).astype(F32).astype(BF16)
 
     pl.semaphore_wait(barrier, greeted)
 
@@ -185,6 +184,10 @@
             yy, xx = in_column(dy, dx)
             send(idx_own.at[yy], idx_all.at[j], 1, device(yy, z, xx))
 
+    slot = owner * cap + rank
+    place[...] = (iota((slots, tok), 0) == slot).astype(F32).astype(BF16)
+    slot_col = jnp.broadcast_to(slot.astype(F32), (8, tok)).T[:, :1].astype(jnp.int32)
+    unplace = (iota((tok, slots), 1) == slot_col).astype(F32).astype(BF16)
     loads[3].wait()
     loads[4].wait()
     loads[5].wait()

time: 57.4 us -> 57.4 us (level)
  no operation moved by 1% of the time
where the time goes in v5:
time: 57.4 us; the launch traced here: 57.2 us
  Pallas kernels  56.6 us (99%)
  between operations  0.64 us (1%)
    pallas_call x1, Pallas kernels, on_device(): pl.pallas_call(functools.partial(kernel, ny, nz, nx, cap), out_shape=(jax...  54.9 us
    pallas_call x1, Pallas kernels, on_device(): pl.pallas_call(hand_on, out_shape=tuple((jax.ShapeDtypeStruct(r.shape, r....  1.71 us

profile of v5, /device:TPU:1, one launch (start us, length us, event | category | flops | bytes accessed | tf_op | source)
XLA Modules:
  0.0 57.2 jit_solution(1550482388294699451)
XLA Ops:
  0.6 54.9 %hstu.1 = (bf16[256,512]{1,0:T(8,128)(2,1)}, f32[16,512]{1,0:T(8,128)}, bf16[8,512]{1,0:T(8,128)(2,1)}) custom-call(s32[1,256]{1,0:T(1,128)} %bitcast.2, s32[1,256]{1,0:T(1,128)} %bitcast.3, s32[1,2]{1,0:T(1,128)} %len_hbm.1, bf16[1024,512]{1,0:T(8,128)(2,1)} %table_hbm.1, bf16[512,2048]{1,0:T(8,128)(2,1)} %w_in_hbm.1, bf16[512,512]{1,0:T(8,128)(2,1)} %w_out_hbm.1, ...), custom_call_target="tpu_custom_call" | custom-call | tf_op jit(solution)/shard_map/hstu/pallas_call | solution.py:487
  55.5 1.7 %hand_on.1 = (bf16[256,512]{1,0:T(8,128)(2,1)}, f32[16,512]{1,0:T(8,128)}, bf16[8,512]{1,0:T(8,128)(2,1)}) custom-call(bf16[256,512]{1,0:T(8,128)(2,1)} %get-tuple-element.6.refs_0_, f32[16,512]{1,0:T(8,128)} %get-tuple-element.7.refs_1_, bf16[8,512]{1,0:T(8,128)(2,1)} %get-tuple-element.8.refs_2_), custom_call_target="tpu_custom_call" | custom-call | tf_op jit(solution)/shard_map/hand_on/pallas_call | solution.py:510
